TPU v7x, 32 devices: a whole 2x2x4 slice. The times are simulated.
32 devices in a mesh: cfg: 2 (over core), orbit: 8 (over z, y), tp: 2 (over x).
Axes of the slice: x: 2, y: 2, z: 4, core: 2. Of those that a mesh axis runs over, the one named last changes fastest.
Arguments:
- tokens: bfloat16 [2, 8, 1024, 1536], P('cfg', 'orbit', 'tp'), may hold values from -6 to 6
- modulation: float32 [2, 2, 1536], P('cfg'), may hold values from -2 to 6
- w_qkv: bfloat16 [1536, 3, 1536], P(None, None, 'tp'), may hold values from -1 to 1
- w_out: bfloat16 [1536, 1536], P('tp'), may hold values from -0.15625 to 0.15625
- adjacency: int32 [8, 4, 8], P('orbit'), may hold values 0 or 1
Outputs:
- guided: bfloat16 [8, 1024, 1536], P('orbit', 'tp', 'cfg')
All inputs are finite; a program needn't handle non-finite values. No bound on the sum of `adjacency` on one device may be relied on, other than what follows from the above.
Results may differ from a plain program's by a relative error of at most 0.0075.
Values may be sent and summed in bfloat16 or wider, within the bound.
A program may use at most 128 MiB of HBM per device.

v0:
```python
import jax
import jax.numpy as jnp
from jax import lax
from jax.sharding import PartitionSpec as P

HEAD_DIM = 128
REACH = 2


guide_scale = 4.0


def from_behind(array, axis, by):
    count = lax.axis_size(axis)
    return lax.ppermute(array, axis, [(i, (i + by) % count) for i in range(count)])


def attend_head(queries, keyset, valueset, keymask):
    scores = jnp.dot(queries, keyset.T, preferred_element_type=jnp.float32) * queries.shape[1] ** (
        -0.5
    )
    scores = jnp.where(keymask[None, :], scores, -1e30)
    peak = jnp.max(scores, axis=1, keepdims=True)
    expon = jnp.exp(scores - peak)
    total = jnp.sum(expon, axis=1, keepdims=True)
    weights = expon.astype(jnp.bfloat16)
    return (jnp.dot(weights, valueset, preferred_element_type=jnp.float32) / total).astype(
        jnp.bfloat16
    )


def direct_send(payload, amount):
    return from_behind(payload, "orbit", amount)


def per_device(tokens, modulation, w_qkv, w_out, adjacency):
    inputs = tokens[0, 0].astype(jnp.float32)
    width = inputs.shape[1]
    half_heads = w_qkv.shape[2]
    shift_scale = modulation[0]
    squares = jnp.mean(inputs * inputs, axis=1, keepdims=True)
    normed = (inputs * lax.rsqrt(squares + 1e-06) * (1.0 + shift_scale[1]) + shift_scale[0]).astype(
        jnp.bfloat16
    )
    whole = lax.all_gather(normed, "tp", axis=0, tiled=True)
    rows_view = whole.shape[0]
    qkv = jnp.dot(whole, w_qkv.reshape(width, 3 * half_heads), preferred_element_type=jnp.float32)
    qkv = qkv.astype(jnp.bfloat16).reshape(rows_view, 3, half_heads)
    queries = qkv[:, 0]
    own_pair = qkv[:, 1:]
    received = {}
    for offset in range(1, REACH + 1):
        received[offset] = direct_send(own_pair, -offset)
        received[-offset] = direct_send(own_pair, offset)
    received[0] = own_pair
    stacked = jnp.stack([received[offset] for offset in range(-REACH, REACH + 1)], axis=0)
    keyflat = stacked[:, :, 0].reshape((2 * REACH + 1) * rows_view, half_heads)
    valflat = stacked[:, :, 1].reshape((2 * REACH + 1) * rows_view, half_heads)
    flags = adjacency[0]
    blocks = flags.shape[1]
    allowed = jnp.concatenate(
        [flags[:REACH], jnp.ones((1, blocks), jnp.int32), flags[REACH:]], axis=0
    )
    keymask = jnp.repeat(allowed, rows_view // blocks, axis=1).reshape(-1) > 0

    def one_head(head_index):
        start = head_index * HEAD_DIM
        return attend_head(
            lax.dynamic_slice_in_dim(queries, start, HEAD_DIM, 1),
            lax.dynamic_slice_in_dim(keyflat, start, HEAD_DIM, 1),
            lax.dynamic_slice_in_dim(valflat, start, HEAD_DIM, 1),
            keymask,
        )

    heads_out = lax.map(one_head, jnp.arange(half_heads // HEAD_DIM, dtype=jnp.int32))
    context = jnp.transpose(heads_out, (1, 0, 2)).reshape(rows_view, half_heads)
    summed = lax.psum_scatter(
        jnp.dot(context, w_out, preferred_element_type=jnp.float32),
        "tp",
        scatter_dimension=0,
        tiled=True,
    )
    branch_out = summed.astype(jnp.bfloat16)
    owner = lax.axis_index("cfg")
    half_width = width // 2
    weight_now = jnp.where(owner == 0, guide_scale, 1.0 - guide_scale).astype(jnp.float32)
    combined = lax.psum(
        (weight_now * branch_out.astype(jnp.float32)).astype(jnp.bfloat16), "cfg"
    ).astype(jnp.float32)
    guided = lax.dynamic_slice_in_dim(combined, owner * half_width, half_width, 1)
    return guided.astype(jnp.bfloat16)[None]


def solution(mesh):
    return jax.shard_map(
        per_device,
        mesh=mesh,
        in_specs=(
            P("cfg", "orbit", "tp", None),
            P("cfg", None, None),
            P(None, None, "tp"),
            P("tp", None),
            P("orbit", None, None),
        ),
        out_specs=P("orbit", "tp", "cfg"),
        check_vma=False,
    )
```

profile of v0, /device:TPU:1, one launch (start us, length us, event | category | flops | bytes accessed | tf_op | source)
XLA Modules:
  0.0 539.9 jit_solution(17024833661529500961)
XLA Ops:
  12.5 10.3 %copy.7 = bf16[1536,3,768]{0,2,1:T(8,128)(2,1)} copy(bf16[1536,3,768]{2,0,1:T(8,128)(2,1)} %param.9) | data formatting | bytes 14155776 | tf_op args[2]
  22.8 36.8 %all-gather.2.cloned.1.call-done = bf16[1024,1536]{1,0:T(8,128)(2,1)} async-done(((bf16[512,1536]{1,0:T(8,128)(2,1)}), bf16[1024,1536]{1,0:T(8,128)(2,1)}) %all-gather.2.cloned.1.call-update) | async-done | bytes 3145744 | tf_op jit(solution)/shard_map/all_gather | solution.py:45
  59.6 12.6 %convolution_convert_fusion = bf16[1024,2304]{1,0:T(8,128)(2,1)} fusion(bf16[1024,1536]{1,0:T(8,128)(2,1)} %all-gather.2.cloned.1.call-done, bf16[1536,2304]{0,1:T(8,128)(2,1)} %bitcast.52), kind=kOutput, calls=%fused_computation.21 | convolution fusion | flops 7250116608 | bytes 14942208 | tf_op jit(solution)/shard_map/dot_general | solution.py:47
  72.2 6.6 %copy.8 = bf16[1024,2304]{0,1:T(8,128)(2,1)} copy(bf16[1024,2304]{1,0:T(8,128)(2,1)} %convolution_convert_fusion) | data formatting | bytes 9437184 | tf_op jit(solution)/shard_map/convert_element_type | solution.py:48
  91.3 62.5 %collective-permute-done = bf16[1024,2,768]{0,2,1:T(8,128)(2,1)} collective-permute-done((bf16[1024,2,768]{0,2,1:T(8,128)(2,1)}, bf16[1024,2,768]{0,2,1:T(8,128)(2,1)}, u32[]{:S(2)}, u32[]{:S(2)}) %collective-permute-start) | collective-permute-done | bytes 3145760 | tf_op jit(solution)/shard_map/ppermute | solution.py:15
  156.1 66.1 %collective-permute-done.1 = bf16[1024,2,768]{0,2,1:T(8,128)(2,1)} collective-permute-done((bf16[1024,2,768]{0,2,1:T(8,128)(2,1)}, bf16[1024,2,768]{0,2,1:T(8,128)(2,1)}, u32[]{:S(2)}, u32[]{:S(2)}) %collective-permute-start.1) | collective-permute-done | bytes 3145760 | tf_op jit(solution)/shard_map/ppermute | solution.py:15
  226.9 62.8 %collective-permute-done.3 = bf16[1024,2,768]{0,2,1:T(8,128)(2,1)} collective-permute-done((bf16[1024,2,768]{0,2,1:T(8,128)(2,1)}, bf16[1024,2,768]{0,2,1:T(8,128)(2,1)}, u32[]{:S(2)}, u32[]{:S(2)}) %collective-permute-start.3) | collective-permute-done | bytes 3145760 | tf_op jit(solution)/shard_map/ppermute | solution.py:15
  291.9 6.0 %fusion.36 = (bf16[5,1024,1,768]{1,3,2,0:T(8,128)(2,1)}, bf16[5,1024,1,768]{1,3,2,0:T(8,128)(2,1)}) fusion(bf16[5,1024,2,768]{1,3,2,0:T(8,128)(2,1)S(1)} %bitcast_dynamic-update-slice_fusion), kind=kLoop, calls=%fused_computation.43 | loop fusion | bytes 31457280 | tf_op jit(solution)/shard_map/slice | solution.py:58
  297.9 10.6 %copy.9 = bf16[5,1024,1,768]{3,1,0,2:T(8,128)(2,1)} copy(bf16[5,1024,1,768]{1,3,2,0:T(8,128)(2,1)} %get-tuple-element.86) | data formatting | bytes 15728640 | tf_op jit(solution)/shard_map/slice | solution.py:57
  308.5 10.5 %copy.10 = bf16[5,1024,1,768]{3,1,0,2:T(8,128)(2,1)} copy(bf16[5,1024,1,768]{1,3,2,0:T(8,128)(2,1)} %get-tuple-element.85) | data formatting | bytes 15728640 | tf_op jit(solution)/shard_map/slice | solution.py:58
  319.0 106.5 %while.11 = (s32[]{:T(128)}, bf16[6,1024,128]{1,2,0:T(8,128)(2,1)}, s32[6]{0:T(128)S(1)}, bf16[1024,768]{0,1:T(8,128)(2,1)}, bf16[5120,768]{1,0:T(8,128)(2,1)}, ...) while((s32[]{:T(128)}, bf16[6,1024,128]{1,2,0:T(8,128)(2,1)}, ...), condition=%wide.region_4.5_spmd.clone, body=%wide.region_1.4_spmd.clone.sunk | while | flops 2742286336 | bytes 67151568 | solution.py:75
  320.5 4.9 fusion.49
  325.4 5.1 fusion.50
  330.5 5.4 %fusion.51 = bf16[1,1024,128]{2,1,0:T(8,128)(2,1)S(1)} fusion(bf16[5120,768]{1,0:T(8,128)(2,1)} %get-tuple-element.163, s32[]{:T(128)S(6)} %select_n.43, f32[1024,5120]{1,0:T(8,128)S(1)} %get-tuple-element.134, f32[1024]{0:T(1024)S(1)} %get-tuple-element.135, pred[5120]{0:T(1024)(128)(4,1)S(1)} %broadcast_bitcast_fusion.2, f32[1024]{0:T(1024)S(1)} %fusion.50), kind=kOutput, calls=%fused_computation.13.clone.1 | convolution fusion | flops 1363410944 | bytes 22557700 | tf_op jit(solution)/shard_map/while/body/eval_jaxpr/dot_general | solution.py:27
  338.2 4.9 fusion.49
  343.1 5.1 fusion.50
  348.2 5.4 %fusion.51 = bf16[1,1024,128]{2,1,0:T(8,128)(2,1)S(1)} fusion(bf16[5120,768]{1,0:T(8,128)(2,1)} %get-tuple-element.163, s32[]{:T(128)S(6)} %select_n.43, f32[1024,5120]{1,0:T(8,128)S(1)} %get-tuple-element.134, f32[1024]{0:T(1024)S(1)} %get-tuple-element.135, pred[5120]{0:T(1024)(128)(4,1)S(1)} %broadcast_bitcast_fusion.2, f32[1024]{0:T(1024)S(1)} %fusion.50), kind=kOutput, calls=%fused_computation.13.clone.1 | convolution fusion | flops 1363410944 | bytes 22557700 | tf_op jit(solution)/shard_map/while/body/eval_jaxpr/dot_general | solution.py:27
  356.0 4.9 fusion.49
  360.9 5.1 fusion.50
  366.0 5.4 %fusion.51 = bf16[1,1024,128]{2,1,0:T(8,128)(2,1)S(1)} fusion(bf16[5120,768]{1,0:T(8,128)(2,1)} %get-tuple-element.163, s32[]{:T(128)S(6)} %select_n.43, f32[1024,5120]{1,0:T(8,128)S(1)} %get-tuple-element.134, f32[1024]{0:T(1024)S(1)} %get-tuple-element.135, pred[5120]{0:T(1024)(128)(4,1)S(1)} %broadcast_bitcast_fusion.2, f32[1024]{0:T(1024)S(1)} %fusion.50), kind=kOutput, calls=%fused_computation.13.clone.1 | convolution fusion | flops 1363410944 | bytes 22557700 | tf_op jit(solution)/shard_map/while/body/eval_jaxpr/dot_general | solution.py:27
  373.7 4.9 fusion.49
  378.6 5.1 fusion.50
  383.7 5.4 %fusion.51 = bf16[1,1024,128]{2,1,0:T(8,128)(2,1)S(1)} fusion(bf16[5120,768]{1,0:T(8,128)(2,1)} %get-tuple-element.163, s32[]{:T(128)S(6)} %select_n.43, f32[1024,5120]{1,0:T(8,128)S(1)} %get-tuple-element.134, f32[1024]{0:T(1024)S(1)} %get-tuple-element.135, pred[5120]{0:T(1024)(128)(4,1)S(1)} %broadcast_bitcast_fusion.2, f32[1024]{0:T(1024)S(1)} %fusion.50), kind=kOutput, calls=%fused_computation.13.clone.1 | convolution fusion | flops 1363410944 | bytes 22557700 | tf_op jit(solution)/shard_map/while/body/eval_jaxpr/dot_general | solution.py:27
  391.5 4.9 fusion.49
  396.4 5.1 fusion.50
  401.5 5.4 %fusion.51 = bf16[1,1024,128]{2,1,0:T(8,128)(2,1)S(1)} fusion(bf16[5120,768]{1,0:T(8,128)(2,1)} %get-tuple-element.163, s32[]{:T(128)S(6)} %select_n.43, f32[1024,5120]{1,0:T(8,128)S(1)} %get-tuple-element.134, f32[1024]{0:T(1024)S(1)} %get-tuple-element.135, pred[5120]{0:T(1024)(128)(4,1)S(1)} %broadcast_bitcast_fusion.2, f32[1024]{0:T(1024)S(1)} %fusion.50), kind=kOutput, calls=%fused_computation.13.clone.1 | convolution fusion | flops 1363410944 | bytes 22557700 | tf_op jit(solution)/shard_map/while/body/eval_jaxpr/dot_general | solution.py:27
  409.2 4.9 fusion.49
  414.1 5.1 fusion.50
  419.2 5.4 %fusion.51 = bf16[1,1024,128]{2,1,0:T(8,128)(2,1)S(1)} fusion(bf16[5120,768]{1,0:T(8,128)(2,1)} %get-tuple-element.163, s32[]{:T(128)S(6)} %select_n.43, f32[1024,5120]{1,0:T(8,128)S(1)} %get-tuple-element.134, f32[1024]{0:T(1024)S(1)} %get-tuple-element.135, pred[5120]{0:T(1024)(128)(4,1)S(1)} %broadcast_bitcast_fusion.2, f32[1024]{0:T(1024)S(1)} %fusion.50), kind=kOutput, calls=%fused_computation.13.clone.1 | convolution fusion | flops 1363410944 | bytes 22557700 | tf_op jit(solution)/shard_map/while/body/eval_jaxpr/dot_general | solution.py:27
  425.5 6.1 %fusion.37 = f32[1024,1536]{1,0:T(8,128)} fusion(bf16[1024,768]{0,1:T(8,128)(2,1)} %bitcast.53, bf16[768,1536]{1,0:T(8,128)(2,1)S(1)} %copy-done), kind=kOutput, calls=%fused_computation.44 | convolution fusion | flops 2415919104 | bytes 10223616 | tf_op jit(solution)/shard_map/dot_general | solution.py:78
  431.7 75.2 %reduce-scatter.2.cloned.1.call-done = f32[512,1536]{1,0:T(8,128)} async-done(((f32[1024,1536]{1,0:T(8,128)}), f32[512,1536]{1,0:T(8,128)}) %reduce-scatter.2.cloned.1.call-update) | async-done | bytes 3145744 | tf_op jit(solution)/shard_map/reduce_scatter | solution.py:77
  510.4 20.9 %all-reduce.2.cloned.1.call-done = bf16[512,1536]{1,0:T(8,128)(2,1)} async-done(((bf16[512,1536]{1,0:T(8,128)(2,1)}), bf16[512,1536]{1,0:T(8,128)(2,1)}) %all-reduce.2.cloned.1.call-update) | async-done | bytes 1572880 | tf_op jit(solution)/shard_map/psum | solution.py:87
  (62 shorter events, 42.7 us)
Async XLA Ops:
  6.5 419.0 %copy-start = (bf16[768,1536]{1,0:T(8,128)(2,1)S(1)}, bf16[768,1536]{1,0:T(8,128)(2,1)}, u32[]{:S(2)}) copy-start(bf16[768,1536]{1,0:T(8,128)(2,1)} %param.10) | copy-start | bytes 7077892
  6.5 53.0 %all-gather.2.cloned.1.call-start = ((), (), s32[]{:S(2)}) async-start(), calls=%async_computation.1 | async-start | bytes 4718592 | tf_op jit(solution)/shard_map/all_gather | solution.py:45
  12.4 494.5 %reduce-scatter.2.cloned.1.call-start = ((), (), s32[]{:S(2)}) async-start(), calls=%async_computation.2 | async-start | bytes 9437184 | tf_op jit(solution)/shard_map/reduce_scatter | solution.py:77
  78.8 9.6 %copy-start.1 = (s32[1,4,8]{2,1,0:T(4,128)S(1)}, s32[1,4,8]{2,1,0:T(4,128)}, u32[]{:S(2)}) copy-start(s32[1,4,8]{2,1,0:T(4,128)} %param.11) | copy-start | bytes 388
  82.7 71.1 %collective-permute-start = (bf16[1024,2,768]{0,2,1:T(8,128)(2,1)}, bf16[1024,2,768]{0,2,1:T(8,128)(2,1)}, u32[]{:S(2)}, u32[]{:S(2)}) collective-permute-start(bf16[1024,2,768]{0,2,1:T(8,128)(2,1)} %slice.43), channel_id=1, source_target_pairs={{0,4},{2,6},{4,8},{6,10},{8,12},{10,14},{12,0},{14,2},{1,5},{3,7},... | collective-permute-start | bytes 9437192 | tf_op jit(solution)/shard_map/ppermute | solution.py:15
  83.9 138.3 %collective-permute-start.1 = (bf16[1024,2,768]{0,2,1:T(8,128)(2,1)}, bf16[1024,2,768]{0,2,1:T(8,128)(2,1)}, u32[]{:S(2)}, u32[]{:S(2)}) collective-permute-start(bf16[1024,2,768]{0,2,1:T(8,128)(2,1)} %slice.43), channel_id=1, source_target_pairs={{0,2},{2,4},{4,6},{6,8},{8,10},{10,12},{12,14},{14,0},{1,3},{3,5},... | collective-permute-start | bytes 9437192 | tf_op jit(solution)/shard_map/ppermute | solution.py:15
  85.1 139.6 %collective-permute-start.2 = (bf16[1024,2,768]{0,2,1:T(8,128)(2,1)}, bf16[1024,2,768]{0,2,1:T(8,128)(2,1)}, u32[]{:S(2)}, u32[]{:S(2)}) collective-permute-start(bf16[1024,2,768]{0,2,1:T(8,128)(2,1)} %slice.43), channel_id=1, source_target_pairs={{0,14},{2,0},{4,2},{6,4},{8,6},{10,8},{12,10},{14,12},{1,15},{3,1}... | collective-permute-start | bytes 9437192 | tf_op jit(solution)/shard_map/ppermute | solution.py:15
  88.1 201.6 %collective-permute-start.3 = (bf16[1024,2,768]{0,2,1:T(8,128)(2,1)}, bf16[1024,2,768]{0,2,1:T(8,128)(2,1)}, u32[]{:S(2)}, u32[]{:S(2)}) collective-permute-start(bf16[1024,2,768]{0,2,1:T(8,128)(2,1)} %slice.43), channel_id=1, source_target_pairs={{0,12},{2,14},{4,0},{6,2},{8,4},{10,6},{12,8},{14,10},{1,13},{3,15... | collective-permute-start | bytes 9437192 | tf_op jit(solution)/shard_map/ppermute | solution.py:15
  88.5 135.9 %slice-start = ((s8[4718592]{0:T(1024)(128)(4,1)}), s8[4194304]{0:T(1024)(128)(4,1)S(1)}, s32[]{:S(2)}) async-start(s8[4718592]{0:T(1024)(128)(4,1)} %bitcast.47), calls=%async_computation.4 | async-start | bytes 8388608
  91.3 133.0 %slice-start.1 = ((s8[4718592]{0:T(1024)(128)(4,1)}), s8[524288]{0:T(1024)(128)(4,1)S(1)}, s32[]{:S(2)}) async-start(s8[4718592]{0:T(1024)(128)(4,1)} %bitcast.47), calls=%async_computation.5 | async-start | bytes 1048576
  431.7 99.6 %all-reduce.2.cloned.1.call-start = ((), (), s32[]{:S(2)}) async-start(), calls=%async_computation.3 | async-start | bytes 3145728 | tf_op jit(solution)/shard_map/psum | solution.py:87
Sparse Core Ops, SparseCore 0:
  12.5 46.9 all-gather.1
  431.8 75.1 reduce-scatter.1
  510.5 20.7 all-reduce.1
where the time goes:
time: 542 us; the launch traced here: 540 us
  waiting for transfers between devices  324 us (60%)
  matrix products  80.6 us (15%)
  local copies, waits for them, and re-layouts  69.7 us (13%)
  other arithmetic  41.9 us (8%)
  between operations  13.2 us (2%)
  starting transfers between devices  5.71 us (1%)
    ppermute x4, waiting for transfers between devices, from_behind(): lax.ppermute(array, axis, [(i, (i + by) % count) for i in range(count)])  191 us
    reduce_scatter x1, waiting for transfers between devices, per_device(): lax.psum_scatter(jnp.dot(context, w_out, preferred_element_type=jnp.float...  75.2 us
    all_gather x1, waiting for transfers between devices, per_device(): whole = lax.all_gather(normed, 'tp', axis=0, tiled=True)  36.8 us
    dot_general x6, matrix products, attend_head(): jnp.dot(weights, valueset, preferred_element_type=jnp.float32) / total  32.6 us
    reduce_sum x6, other arithmetic, attend_head(): total = jnp.sum(expon, axis=1, keepdims=True)  30.5 us
    dot_general x6, matrix products, attend_head(): jnp.dot(queries, keyset.T, preferred_element_type=jnp.float32)  29.3 us
    psum x1, waiting for transfers between devices, per_device(): lax.psum((weight_now * branch_out.astype(jnp.float32)).astype(jnp.bfloat1...  20.9 us
    unnamed x13, local copies, waits for them, and re-layouts  17.2 us
  transfers between devices with their start and end apart: 7, of which 6 were waited for; matrix products, arithmetic and copies ran while one was open for 4% of the time, Pallas kernels for 0%

commit v1 on v0

v1 whole, which is shorter than its diff:
```python
import functools
import math

import jax
import jax.numpy as jnp
from jax import lax
from jax.experimental import pallas as pl
from jax.experimental.pallas import tpu as pltpu
from jax.sharding import PartitionSpec as P

HEAD_DIM = 128
REACH = 2
GUIDE = 4.0
MESH = pl.DeviceIdType.MESH
SLOTS = 2 * REACH + 1
TILE = 256
NEG = -1e30


def kernel(
    views,
    tok,
    mod,
    wq,
    wk,
    wv,
    wo,
    bias,
    out,
    xn,
    kv,
    q,
    acc,
    peak,
    wo_far,
    ctx,
    ctx_send,
    ctx_far,
    mix_send,
    mix_far,
    gather_sem,
    wo_sem,
    up_send,
    up_recv,
    down_send,
    down_recv,
    side_send,
    side_recv,
    relay_send,
    relay_recv,
    ctx_ssem,
    ctx_rsem,
    mix_sem,
):
    c = lax.axis_index("cfg")
    v = lax.axis_index("orbit")
    t = lax.axis_index("tp")
    half, width = xn.shape[1], xn.shape[2]
    heads = q.shape[0]
    chunks = 2 * heads
    odd = lax.rem(v, 2)
    mate = (c, v, 1 - t)
    up = (c, lax.rem(v + 2, views), t)
    down = (c, lax.rem(v + views - 2, views), t)
    side = (c, v + 1 - 2 * odd, t)
    core = (1 - c, v, t)

    barrier = pltpu.get_barrier_semaphore()
    for other in (mate, up, down, side, core):
        pl.semaphore_signal(barrier, inc=1, device_id=other, device_id_type=MESH)
    pl.semaphore_wait(barrier, 5)

    def remote(src, dst, ssem, rsem, dev):
        return pltpu.make_async_remote_copy(
            src_ref=src, dst_ref=dst, send_sem=ssem, recv_sem=rsem, device_id=dev, device_id_type=MESH
        )

    def up_copy(i):
        return remote(kv.at[0, i], kv.at[1, i], up_send.at[i], up_recv.at[i], up)

    def down_copy(i):
        return remote(kv.at[0, i], kv.at[2, i], down_send.at[i], down_recv.at[i], down)

    def side_copy(i):
        return remote(kv.at[0, i], kv.at[3, i], side_send.at[i], side_recv.at[i], side)

    def relay_copy(i):
        return remote(kv.at[2 - odd, i], kv.at[4, i], relay_send.at[i], relay_recv.at[i], side)

    def ctx_copy(n):
        cols = pl.ds(pl.multiple_of(n * HEAD_DIM, HEAD_DIM), HEAD_DIM)
        return remote(ctx_send.at[n], ctx_far.at[:, cols], ctx_ssem.at[n], ctx_rsem.at[n], mate)

    shift = mod[0:1, :]
    gain = 1.0 + mod[1:2, :]

    @pl.loop(0, half // 64)
    def _(r):
        rows = pl.ds(pl.multiple_of(r * 64, 64), 64)
        x = tok[rows, :].astype(jnp.float32)
        sq = jnp.mean(x * x, axis=1, keepdims=True)
        xn[0, rows, :] = (x * lax.rsqrt(sq + 1e-06) * gain + shift).astype(jnp.bfloat16)

    gather = remote(xn.at[0], xn.at[1], gather_sem.at[0], gather_sem.at[1], mate)
    gather.start()
    swap_wo = remote(wo, wo_far, wo_sem.at[0], wo_sem.at[1], mate)

    def project_kv(h, with_side):
        @pl.loop(0, heads)
        def _(n):
            cols = pl.ds(pl.multiple_of(n * HEAD_DIM, HEAD_DIM), HEAD_DIM)
            w = jnp.concatenate([wk[:, cols], wv[:, cols]], axis=1)
            i = h * heads + n

            r = jnp.dot(xn[h], w, preferred_element_type=jnp.float32).astype(jnp.bfloat16)
            kv[0, i, 0] = r[:, :HEAD_DIM]
            kv[0, i, 1] = r[:, HEAD_DIM:]
            up_copy(i).start()
            down_copy(i).start()
            if with_side:
                side_copy(i).start()

    def project_q(h):
        @pl.loop(0, heads // 2)
        def _(m):
            cols = pl.ds(pl.multiple_of(m * 2 * HEAD_DIM, 2 * HEAD_DIM), 2 * HEAD_DIM)
            r = jnp.dot(xn[h], wq[:, cols], preferred_element_type=jnp.float32)
            r = (r * (HEAD_DIM**-0.5 / math.log(2.0))).astype(jnp.bfloat16)
            rows = pl.ds(h * half, half)
            q[2 * m, rows, :] = r[:, :HEAD_DIM]
            q[2 * m + 1, rows, :] = r[:, HEAD_DIM:]

    project_kv(0, True)
    project_q(0)
    acc[...] = jnp.zeros_like(acc)
    peak[...] = jnp.full_like(peak, NEG)
    gather.wait_recv()
    project_kv(1, False)
    project_q(1)
    swap_wo.start()

    ones = jnp.ones((half, HEAD_DIM), jnp.bfloat16)

    def pass_on(i):
        up_copy(i).wait_recv()
        down_copy(i).wait_recv()
        relay_copy(i).start()

        @pl.when(i < heads)
        def _():
            side_copy(i + heads).start()

    pass_on(0)

    @pl.loop(0, chunks)
    def _(i):
        h = i // heads
        n = lax.rem(i, heads)

        @pl.when(i + 1 < chunks)
        def _():
            pass_on(i + 1)

        side_copy(i).wait_recv()
        relay_copy(i).wait_recv()

        @pl.loop(0, 2 * half // TILE)
        def _(r):
            rows = pl.ds(pl.multiple_of(r * TILE, TILE), TILE)
            queries = q[n, rows, :]
            scores = []
            for s in range(SLOTS):
                one = lax.dot_general(
                    queries,
                    kv[s, i, 0],
                    (((1,), (1,)), ((), ())),
                    preferred_element_type=jnp.float32,
                )
                if s > 0:
                    one = one + bias[s - 1, h]
                scores.append(one)
            top = scores[0]
            for s in range(1, SLOTS):
                top = jnp.maximum(top, scores[s])
            before = peak[n, rows, :1]
            now = jnp.maximum(before, jnp.max(top, axis=1, keepdims=True))
            total = acc[n, rows, :] * jnp.exp2(before - now)
            for s in range(SLOTS):
                weights = jnp.exp2(scores[s] - now).astype(jnp.bfloat16)
                total = total + jnp.dot(
                    weights,
                    jnp.concatenate([kv[s, i, 1], ones], axis=1),
                    preferred_element_type=jnp.float32,
                )
            acc[n, rows, :] = total
            peak[n, rows, :] = jnp.broadcast_to(now, (TILE, HEAD_DIM))

        @pl.when(h == 1)
        def _():
            def context(start):
                a = acc[n, pl.ds(start, half), :]
                return (a[:, :HEAD_DIM] / a[:, HEAD_DIM:]).astype(jnp.bfloat16)

            ctx_send[n] = context(half)
            ctx_copy(n).start()
            cols = pl.ds(pl.multiple_of(n * HEAD_DIM, HEAD_DIM), HEAD_DIM)
            ctx[:, cols] = context(0)

    swap_wo.wait_recv()
    for n in range(heads):
        ctx_copy(n).wait_recv()

    mine = pl.multiple_of(c * (width // 2), HEAD_DIM)
    others = pl.multiple_of((1 - c) * (width // 2), HEAD_DIM)

    def project_out(start, dst):
        @pl.loop(0, half // TILE)
        def _(r):
            rows = pl.ds(pl.multiple_of(r * TILE, TILE), TILE)
            cols = pl.ds(start, width // 2)
            y = jnp.dot(ctx[rows, :], wo[:, cols], preferred_element_type=jnp.float32)
            y = y + jnp.dot(ctx_far[rows, :], wo_far[:, cols], preferred_element_type=jnp.float32)
            dst[rows, :] = y.astype(jnp.bfloat16)

    project_out(others, mix_send)
    mix = remote(mix_send, mix_far, mix_sem.at[0], mix_sem.at[1], core)
    mix.start()
    project_out(mine, out)
    mix.wait_recv()
    own_scale = jnp.where(c == 0, GUIDE, 1.0 - GUIDE).astype(jnp.float32)

    @pl.loop(0, half // 64)
    def _(r):
        rows = pl.ds(pl.multiple_of(r * 64, 64), 64)
        a = out[rows, :].astype(jnp.float32) * own_scale
        b = mix_far[rows, :].astype(jnp.float32) * (1.0 - own_scale)
        out[rows, :] = (a + b).astype(jnp.bfloat16)

    gather.wait_send()
    swap_wo.wait_send()
    mix.wait_send()

    @pl.loop(0, chunks)
    def _(i):
        up_copy(i).wait_send()
        down_copy(i).wait_send()
        side_copy(i).wait_send()
        relay_copy(i).wait_send()

    @pl.loop(0, heads)
    def _(n):
        ctx_copy(n).wait_send()


def per_device(views, tokens, modulation, w_qkv, w_out, adjacency):
    tok = tokens[0, 0]
    half, width = tok.shape
    part = w_qkv.shape[2]
    heads = part // HEAD_DIM
    chunks = 2 * heads
    odd = lax.axis_index("orbit") % 2
    t = lax.axis_index("tp")
    flags = adjacency[0]
    near, far = flags[1], flags[2]
    order = jnp.stack(
        [flags[0], flags[3], jnp.where(odd == 1, near, far), jnp.where(odd == 1, far, near)]
    )
    keep = jnp.repeat(order, 2 * half // flags.shape[1], axis=1).reshape(4, 2, 1, half)
    keep = jnp.where(t == 0, keep, keep[:, ::-1])
    bias = jnp.where(keep > 0, 0.0, NEG).astype(jnp.float32)
    vmem = pl.BlockSpec(memory_space=pltpu.VMEM)
    bf16, f32 = jnp.bfloat16, jnp.float32
    dma = pltpu.SemaphoreType.DMA
    result = pl.pallas_call(
        functools.partial(kernel, views),
        out_shape=jax.ShapeDtypeStruct((half, width // 2), bf16),
        in_specs=[vmem] * 7,
        out_specs=vmem,
        scratch_shapes=[
            pltpu.VMEM((2, half, width), bf16),
            pltpu.VMEM((SLOTS, chunks, 2, half, HEAD_DIM), bf16),
            pltpu.VMEM((heads, 2 * half, HEAD_DIM), bf16),
            pltpu.VMEM((heads, 2 * half, 2 * HEAD_DIM), f32),
            pltpu.VMEM((heads, 2 * half, HEAD_DIM), f32),
            pltpu.VMEM((part, width), bf16),
            pltpu.VMEM((half, part), bf16),
            pltpu.VMEM((heads, half, HEAD_DIM), bf16),
            pltpu.VMEM((half, part), bf16),
            pltpu.VMEM((half, width // 2), bf16),
            pltpu.VMEM((half, width // 2), bf16),
            dma((2,)),
            dma((2,)),
        ]
        + [dma((chunks,))] * 8
        + [dma((heads,))] * 2
        + [dma((2,))],
        compiler_params=pltpu.CompilerParams(
            collective_id=0, has_side_effects=True, vmem_limit_bytes=62 * 1024 * 1024
        ),
        cost_estimate=pl.CostEstimate(
            flops=26_000_000_000, bytes_accessed=16_000_000, transcendentals=32_000_000
        ),
    )(tok, modulation[0], w_qkv[:, 0], w_qkv[:, 1], w_qkv[:, 2], w_out, bias)
    return result[None]


def solution(mesh):
    return jax.shard_map(
        functools.partial(per_device, mesh.shape["orbit"]),
        mesh=mesh,
        in_specs=(
            P("cfg", "orbit", "tp", None),
            P("cfg", None, None),
            P(None, None, "tp"),
            P("tp", None),
            P("orbit", None, None),
        ),
        out_specs=P("orbit", "tp", "cfg"),
        check_vma=False,
    )
```

time: 542 us -> 191 us (0.35)
  waiting for transfers between devices: 324 us -> 0 us
  Pallas kernels: 0 us -> 181 us
  matrix products: 80.6 us -> 0 us
  local copies, waits for them, and re-layouts: 69.7 us -> 8.23 us
  other arithmetic: 41.9 us -> 1.47 us
  between operations: 13.2 us -> 0.01 us
  starting transfers between devices: 5.71 us -> 0 us
    ppermute x4 -> x0, waiting for transfers between devices: 191 us -> none  [from_behind(): lax.ppermute(array, axis, [(i, (i + by) % count) for i in range(count)])]
    pallas_call x0 -> x1, Pallas kernels: none -> 181 us  [per_device(): pl.pallas_call(functools.partial(kernel, views), out_shape=jax.ShapeDtype...]
    dot_general x14 -> x0, matrix products: 80.6 us -> none  [the longest x6 32.6 us: attend_head(): jnp.dot(weights, valueset, preferred_element_type=jnp.float32) / total]
    reduce_scatter x1 -> x0, waiting for transfers between devices: 75.2 us -> none  [per_device(): lax.psum_scatter(jnp.dot(context, w_out, preferred_element_type=jnp.float...]
    all_gather x1 -> x0, waiting for transfers between devices: 36.8 us -> none  [per_device(): whole = lax.all_gather(normed, 'tp', axis=0, tiled=True)]
    reduce_sum x7 -> x0, other arithmetic: 32.3 us -> none  [the longest x6 30.5 us: attend_head(): total = jnp.sum(expon, axis=1, keepdims=True)]
    slice x5 -> x0, local copies, waits for them, and re-layouts: 31 us -> none  [the longest x2 16.5 us: per_device(): valflat = stacked[:, :, 1].reshape((2 * REACH + 1) * rows_view, half_heads)]
    psum x1 -> x0, waiting for transfers between devices: 20.9 us -> none  [per_device(): lax.psum((weight_now * branch_out.astype(jnp.float32)).astype(jnp.bfloat1...]
  transfers between devices with their start and end apart: 7 -> 0, of which waited for: 6 -> 0; matrix products, arithmetic and copies ran while one was open for 4% -> 0% of each run, Pallas kernels for 0% -> 0%
where the time goes in v1:
time: 191 us
  Pallas kernels  181 us (95%)
  local copies, waits for them, and re-layouts  8.23 us (4%)
    pallas_call x1, Pallas kernels, per_device(): pl.pallas_call(functools.partial(kernel, views), out_shape=jax.ShapeDtype...  181 us
    squeeze x1, local copies, waits for them, and re-layouts, per_device(): w_qkv[:, 2]  6.09 us

profile of v1, /device:TPU:1, one launch (start us, length us, event | category | flops | bytes accessed | tf_op | source)
XLA Modules:
  0.0 191.0 jit_solution(5157840282350962142)
XLA Ops:
  0.0 0.8 slice_bitcast_fusion.4
  0.8 0.1 broadcast_in_dim.14
  0.9 0.6 compare_select_fusion.bias
  1.5 6.1 %slice_bitcast_fusion = (bf16[1536,768]{1,0:T(8,128)(2,1)}, bf16[1536,768]{1,0:T(8,128)(2,1)}, bf16[1536,768]{1,0:T(8,128)(2,1)}) fusion(bf16[1536,3,768]{2,0,1:T(8,128)(2,1)} %param.7), kind=kLoop, calls=%fused_computation | loop fusion | bytes 14155776 | tf_op jit(solution)/shard_map/squeeze | solution.py:303
  7.6 181.3 %shard_map.55 = bf16[512,768]{1,0:T(8,128)(2,1)} custom-call(bf16[512,1536]{1,0:T(8,128)(2,1)} %bitcast.20, f32[2,1536]{1,0:T(2,128)} %bitcast.21, bf16[1536,768]{1,0:T(8,128)(2,1)} %get-tuple-element.6.wq, bf16[1536,768]{1,0:T(8,128)(2,1)} %get-tuple-element.7.wk, bf16[1536,768]{1,0:T(8,128)(2,1)} %get-tuple-element.5.wv, bf16[768,1536]{1,0:T(8,128)(2,1)} %wo.1, ...), custom_call_target="tpu_custom_call" | custom-call | flops 25999998976 | bytes 16000000 | tf_op jit(solution)/shard_map/pallas_call | solution.py:274
  188.9 2.1 %copy.7 = bf16[1,512,768]{2,1,0:T(8,128)(2,1)} copy(bf16[1,512,768]{2,1,0:T(8,128)(2,1)} %bitcast.18) | data formatting | bytes 1572864
  (1 shorter events, 0.0 us)

commit v2 on v1

--- a/solution.py
+++ b/solution.py
@@ -21,9 +21,7 @@
     views,
     tok,
     mod,
-    wq,
-    wk,
-    wv,
+    w_all,
     wo,
     bias,
     out,
@@ -109,7 +107,7 @@
         @pl.loop(0, heads)
         def _(n):
             cols = pl.ds(pl.multiple_of(n * HEAD_DIM, HEAD_DIM), HEAD_DIM)
-            w = jnp.concatenate([wk[:, cols], wv[:, cols]], axis=1)
+            w = jnp.concatenate([w_all[1, :, cols], w_all[2, :, cols]], axis=1)
             i = h * heads + n
 
             r = jnp.dot(xn[h], w, preferred_element_type=jnp.float32).astype(jnp.bfloat16)
@@ -124,7 +122,7 @@
         @pl.loop(0, heads // 2)
         def _(m):
             cols = pl.ds(pl.multiple_of(m * 2 * HEAD_DIM, 2 * HEAD_DIM), 2 * HEAD_DIM)
-            r = jnp.dot(xn[h], wq[:, cols], preferred_element_type=jnp.float32)
+            r = jnp.dot(xn[h], w_all[0, :, cols], preferred_element_type=jnp.float32)
             r = (r * (HEAD_DIM**-0.5 / math.log(2.0))).astype(jnp.bfloat16)
             rows = pl.ds(h * half, half)
             q[2 * m, rows, :] = r[:, :HEAD_DIM]
@@ -164,7 +162,7 @@
         side_copy(i).wait_recv()
         relay_copy(i).wait_recv()
 
-        @pl.loop(0, 2 * half // TILE)
+        @pl.loop(0, 2 * half // TILE, unroll=4)
         def _(r):
             rows = pl.ds(pl.multiple_of(r * TILE, TILE), TILE)
             queries = q[n, rows, :]
@@ -274,7 +272,7 @@
     result = pl.pallas_call(
         functools.partial(kernel, views),
         out_shape=jax.ShapeDtypeStruct((half, width // 2), bf16),
-        in_specs=[vmem] * 7,
+        in_specs=[vmem] * 5,
         out_specs=vmem,
         scratch_shapes=[
             pltpu.VMEM((2, half, width), bf16),
@@ -300,7 +298,7 @@
         cost_estimate=pl.CostEstimate(
             flops=26_000_000_000, bytes_accessed=16_000_000, transcendentals=32_000_000
         ),
-    )(tok, modulation[0], w_qkv[:, 0], w_qkv[:, 1], w_qkv[:, 2], w_out, bias)
+    )(tok, modulation[0], jnp.transpose(w_qkv, (1, 0, 2)), w_out, bias)
     return result[None]
 
 

time: 191 us -> 172 us (0.901)
  Pallas kernels: 181 us -> 168 us
  local copies, waits for them, and re-layouts: 8.23 us -> 2.14 us
    pallas_call x1, Pallas kernels: 181 us -> 168 us  [per_device(): pl.pallas_call(functools.partial(kernel, views), out_shape=jax.ShapeDtype...]
    squeeze x1 -> x0, local copies, waits for them, and re-layouts: 6.09 us -> none  [per_device(): w_qkv[:, 2]]
where the time goes in v2:
time: 172 us
  Pallas kernels  168 us (98%)
  local copies, waits for them, and re-layouts  2.14 us (1%)
    pallas_call x1, Pallas kernels, per_device(): pl.pallas_call(functools.partial(kernel, views), out_shape=jax.ShapeDtype...  168 us

profile of v2, /device:TPU:1, one launch (start us, length us, event | category | flops | bytes accessed | tf_op | source)
XLA Modules:
  0.0 171.7 jit_solution(979107565062280739)
XLA Ops:
  0.0 0.8 slice_bitcast_fusion.1
  0.8 0.1 broadcast_in_dim.14
  0.9 0.6 compare_select_fusion.bias
  1.5 168.0 %shard_map.55 = bf16[512,768]{1,0:T(8,128)(2,1)} custom-call(bf16[512,1536]{1,0:T(8,128)(2,1)} %bitcast.16, f32[2,1536]{1,0:T(2,128)} %bitcast.17, bf16[3,1536,768]{2,1,0:T(8,128)(2,1)} %bitcast.15, bf16[768,1536]{1,0:T(8,128)(2,1)} %wo.1, f32[4,2,1,512]{3,2,1,0:T(1,128)} %compare_select_fusion.bias), custom_call_target="tpu_custom_call" | custom-call | flops 25999998976 | bytes 16000000 | tf_op jit(solution)/shard_map/pallas_call | solution.py:272
  169.6 2.1 %copy.7 = bf16[1,512,768]{2,1,0:T(8,128)(2,1)} copy(bf16[1,512,768]{2,1,0:T(8,128)(2,1)} %bitcast.13) | data formatting | bytes 1572864
  (1 shorter events, 0.0 us)

commit v3 on v2

--- a/solution.py
+++ b/solution.py
@@ -21,10 +21,14 @@
     views,
     tok,
     mod,
+    w_hbm,
+    wo_hbm,
+    flags,
+    out,
     w_all,
     wo,
     bias,
-    out,
+    partial,
     xn,
     kv,
     q,
@@ -49,6 +53,7 @@
     ctx_ssem,
     ctx_rsem,
     mix_sem,
+    load_sem,
 ):
     c = lax.axis_index("cfg")
     v = lax.axis_index("orbit")
@@ -66,7 +71,24 @@
     barrier = pltpu.get_barrier_semaphore()
     for other in (mate, up, down, side, core):
         pl.semaphore_signal(barrier, inc=1, device_id=other, device_id_type=MESH)
-    pl.semaphore_wait(barrier, 5)
+    loads = [
+        pltpu.make_async_copy(w_hbm.at[1], w_all.at[1], load_sem.at[0]),
+        pltpu.make_async_copy(w_hbm.at[2], w_all.at[2], load_sem.at[1]),
+        pltpu.make_async_copy(w_hbm.at[0], w_all.at[0], load_sem.at[2]),
+        pltpu.make_async_copy(wo_hbm, wo, load_sem.at[3]),
+    ]
+    for load in loads:
+        load.start()
+
+    blocks = flags.shape[1]
+    for s in range(SLOTS - 1):
+        row = (0, REACH * 2 - 1, REACH - odd, REACH - 1 + odd)[s]
+        for h in range(2):
+            for b in range(blocks // 2):
+                block = b + (blocks // 2) * lax.rem(h + t, 2)
+                value = jnp.where(flags[row, block] > 0, 0.0, NEG).astype(jnp.float32)
+                size = 2 * half // blocks
+                bias[s, h, :, b * size : (b + 1) * size] = jnp.full((1, size), value, jnp.float32)
 
     def remote(src, dst, ssem, rsem, dev):
         return pltpu.make_async_remote_copy(
@@ -99,6 +121,7 @@
         sq = jnp.mean(x * x, axis=1, keepdims=True)
         xn[0, rows, :] = (x * lax.rsqrt(sq + 1e-06) * gain + shift).astype(jnp.bfloat16)
 
+    pl.semaphore_wait(barrier, 5)
     gather = remote(xn.at[0], xn.at[1], gather_sem.at[0], gather_sem.at[1], mate)
     gather.start()
     swap_wo = remote(wo, wo_far, wo_sem.at[0], wo_sem.at[1], mate)
@@ -128,13 +151,17 @@
             q[2 * m, rows, :] = r[:, :HEAD_DIM]
             q[2 * m + 1, rows, :] = r[:, HEAD_DIM:]
 
+    loads[0].wait()
+    loads[1].wait()
     project_kv(0, True)
+    loads[2].wait()
     project_q(0)
     acc[...] = jnp.zeros_like(acc)
     peak[...] = jnp.full_like(peak, NEG)
     gather.wait_recv()
     project_kv(1, False)
     project_q(1)
+    loads[3].wait()
     swap_wo.start()
 
     ones = jnp.ones((half, HEAD_DIM), jnp.bfloat16)
@@ -158,6 +185,23 @@
         @pl.when(i + 1 < chunks)
         def _():
             pass_on(i + 1)
+
+        @pl.when(i + 1 == chunks)
+        def _():
+            swap_wo.wait_recv()
+            for m in range(heads - 1):
+                ctx_copy(m).wait_recv()
+            known = (heads - 1) * HEAD_DIM
+
+            @pl.loop(0, half // TILE)
+            def _(r):
+                rows = pl.ds(pl.multiple_of(r * TILE, TILE), TILE)
+                for k in range(2):
+                    cols = slice(k * (width // 2), (k + 1) * (width // 2))
+                    y = jnp.dot(ctx[rows, :known], wo[:known, cols], preferred_element_type=jnp.float32)
+                    partial[k, rows, :] = y + jnp.dot(
+                        ctx_far[rows, :known], wo_far[:known, cols], preferred_element_type=jnp.float32
+                    )
 
         side_copy(i).wait_recv()
         relay_copy(i).wait_recv()
@@ -204,26 +248,28 @@
             cols = pl.ds(pl.multiple_of(n * HEAD_DIM, HEAD_DIM), HEAD_DIM)
             ctx[:, cols] = context(0)
 
-    swap_wo.wait_recv()
-    for n in range(heads):
-        ctx_copy(n).wait_recv()
-
+    ctx_copy(heads - 1).wait_recv()
     mine = pl.multiple_of(c * (width // 2), HEAD_DIM)
     others = pl.multiple_of((1 - c) * (width // 2), HEAD_DIM)
 
-    def project_out(start, dst):
+    def project_out(k, start, dst):
         @pl.loop(0, half // TILE)
         def _(r):
             rows = pl.ds(pl.multiple_of(r * TILE, TILE), TILE)
             cols = pl.ds(start, width // 2)
-            y = jnp.dot(ctx[rows, :], wo[:, cols], preferred_element_type=jnp.float32)
-            y = y + jnp.dot(ctx_far[rows, :], wo_far[:, cols], preferred_element_type=jnp.float32)
+            last = slice((heads - 1) * HEAD_DIM, heads * HEAD_DIM)
+            y = jnp.dot(
+                jnp.concatenate([ctx[rows, last], ctx_far[rows, last]], axis=1),
+                jnp.concatenate([wo[last, cols], wo_far[last, cols]], axis=0),
+                preferred_element_type=jnp.float32,
+            )
+            y = y + partial[k, rows, :]
             dst[rows, :] = y.astype(jnp.bfloat16)
 
-    project_out(others, mix_send)
+    project_out(1 - c, others, mix_send)
     mix = remote(mix_send, mix_far, mix_sem.at[0], mix_sem.at[1], core)
     mix.start()
-    project_out(mine, out)
+    project_out(c, mine, out)
     mix.wait_recv()
     own_scale = jnp.where(c == 0, GUIDE, 1.0 - GUIDE).astype(jnp.float32)
 
@@ -256,25 +302,20 @@
     part = w_qkv.shape[2]
     heads = part // HEAD_DIM
     chunks = 2 * heads
-    odd = lax.axis_index("orbit") % 2
-    t = lax.axis_index("tp")
-    flags = adjacency[0]
-    near, far = flags[1], flags[2]
-    order = jnp.stack(
-        [flags[0], flags[3], jnp.where(odd == 1, near, far), jnp.where(odd == 1, far, near)]
-    )
-    keep = jnp.repeat(order, 2 * half // flags.shape[1], axis=1).reshape(4, 2, 1, half)
-    keep = jnp.where(t == 0, keep, keep[:, ::-1])
-    bias = jnp.where(keep > 0, 0.0, NEG).astype(jnp.float32)
     vmem = pl.BlockSpec(memory_space=pltpu.VMEM)
+    anywhere = pl.BlockSpec(memory_space=pl.ANY)
     bf16, f32 = jnp.bfloat16, jnp.float32
     dma = pltpu.SemaphoreType.DMA
     result = pl.pallas_call(
         functools.partial(kernel, views),
         out_shape=jax.ShapeDtypeStruct((half, width // 2), bf16),
-        in_specs=[vmem] * 5,
+        in_specs=[vmem, vmem, anywhere, anywhere, pl.BlockSpec(memory_space=pltpu.SMEM)],
         out_specs=vmem,
         scratch_shapes=[
+            pltpu.VMEM((3, width, part), bf16),
+            pltpu.VMEM((part, width), bf16),
+            pltpu.VMEM((SLOTS - 1, 2, 1, half), f32),
+            pltpu.VMEM((2, half, width // 2), f32),
             pltpu.VMEM((2, half, width), bf16),
             pltpu.VMEM((SLOTS, chunks, 2, half, HEAD_DIM), bf16),
             pltpu.VMEM((heads, 2 * half, HEAD_DIM), bf16),
@@ -291,14 +332,14 @@
         ]
         + [dma((chunks,))] * 8
         + [dma((heads,))] * 2
-        + [dma((2,))],
+        + [dma((2,)), dma((4,))],
         compiler_params=pltpu.CompilerParams(
             collective_id=0, has_side_effects=True, vmem_limit_bytes=62 * 1024 * 1024
         ),
         cost_estimate=pl.CostEstimate(
             flops=26_000_000_000, bytes_accessed=16_000_000, transcendentals=32_000_000
         ),
-    )(tok, modulation[0], jnp.transpose(w_qkv, (1, 0, 2)), w_out, bias)
+    )(tok, modulation[0], jnp.transpose(w_qkv, (1, 0, 2)), w_out, adjacency[0])
     return result[None]
 
 

time: 172 us -> 171 us (level)
  no operation moved by 1% of the time
where the time goes in v3:
time: 171 us; the launch traced here: 170 us
  Pallas kernels  168 us (98%)
  local copies, waits for them, and re-layouts  2.06 us (1%)
    pallas_call x1, Pallas kernels, per_device(): pl.pallas_call(functools.partial(kernel, views), out_shape=jax.ShapeDtype...  168 us

profile of v3, /device:TPU:1, one launch (start us, length us, event | category | flops | bytes accessed | tf_op | source)
XLA Modules:
  0.0 170.4 jit_solution(15498385767269106461)
XLA Ops:
  0.0 168.3 %shard_map.55 = bf16[512,768]{1,0:T(8,128)(2,1)} custom-call(bf16[512,1536]{1,0:T(8,128)(2,1)} %bitcast.7, f32[2,1536]{1,0:T(2,128)} %bitcast.8, bf16[3,1536,768]{2,1,0:T(8,128)(2,1)} %bitcast.6, bf16[768,1536]{1,0:T(8,128)(2,1)} %wo_hbm.1, s32[4,8]{1,0:T(4,128)} %bitcast.9), custom_call_target="tpu_custom_call" | custom-call | flops 25999998976 | bytes 16000000 | tf_op jit(solution)/shard_map/pallas_call | solution.py:309
  168.3 2.1 %copy.7 = bf16[1,512,768]{2,1,0:T(8,128)(2,1)} copy(bf16[1,512,768]{2,1,0:T(8,128)(2,1)} %bitcast.5) | data formatting | bytes 1572864
